TPU v7x, 512 devices: a whole 4x4x16 slice. The times are simulated.
512 devices in a mesh: ctx: 64 (over y_lo, z, core), blk: 8 (over x, y_hi).
Axes of the slice: x: 4, y: 4 (y_hi: 2, y_lo: 2; y = y_hi * 2 + y_lo), z: 16, core: 2. Of those that a mesh axis runs over, the one named last changes fastest.
Arguments:
- queries: bfloat16 [128, 2560], P('blk'), may hold values from -6 to 6, as said below
- keys: bfloat16 [196608, 2560], P(('ctx', 'blk')), may hold values from -6 to 6, as said below
- values: bfloat16 [196608, 2560], P(('ctx', 'blk')), may hold values from -8 to 8, as said below
- offset: int32 [1], replicated, may hold values from 147328 to 196480
- lambdas: float32 [10], replicated, may hold values from 0.2 to 0.8
- gain: float32 [2560], replicated, may hold values from 0.5 to 1.5
Outputs:
- normed: bfloat16 [128, 2560], P('blk')
Inputs may be any that keep to these rules, and one draw needn't show every extreme that they name: `queries`: entries lie in this range. `keys`: entries lie in this range. `values`: entries lie in this range.
All inputs are finite; a program needn't handle non-finite values.
Results may differ from a plain program's by a relative error of at most 0.01.
Values may be sent and summed in bfloat16 or wider, within the bound.
A program may use at most 64 MiB of HBM per device.

v0:
```python
import jax
import jax.numpy as jnp
from jax import lax
from jax.sharding import PartitionSpec as P


def per_device(queries, keys, values, offset, lambdas, gain):
    key_rows = keys.shape[0]
    row_count = queries.shape[0]
    head_count = lambdas.shape[0]
    head_dim = keys.shape[1] // (2 * head_count)
    value_dim = values.shape[1] // head_count
    blk_count = lax.axis_size("blk")
    score_scale = head_dim ** (-0.5)
    key_start = (lax.axis_index("ctx") * blk_count + lax.axis_index("blk")) * key_rows
    key_four = keys.reshape(key_rows, head_count, 2, head_dim)
    value_three = values.reshape(key_rows, head_count, value_dim)
    key_pos = key_start + jnp.arange(key_rows, dtype=jnp.int32)
    query_rows = lax.all_gather(queries, "blk", axis=0, tiled=True)
    rows_here = query_rows.shape[0]
    query_four = query_rows.reshape(rows_here, head_count, 2, head_dim)
    scores = (
        jnp.einsum("rhmd,khmd->hmrk", query_four, key_four, preferred_element_type=jnp.float32)
        * score_scale
    )
    row_pos = offset[0] + jnp.arange(rows_here, dtype=jnp.int32)
    visible = key_pos[None, :] <= row_pos[:, None]
    masked = jnp.where(visible, scores, jnp.float32(-1e30))
    row_max = jnp.max(masked, axis=-1)
    expo = jnp.where(visible, jnp.exp(masked - row_max[..., None]), jnp.float32(0.0))
    row_total = jnp.sum(expo, axis=-1)
    out_sum = jnp.einsum(
        "hmrk,khd->hmrd", expo.astype(jnp.bfloat16), value_three, preferred_element_type=jnp.float32
    )
    out_sum, row_max, row_total = (out_sum, row_max, row_total)
    held_sum = out_sum[None]
    held_max = row_max[None]
    held_total = row_total[None]
    part_sum = lax.all_to_all(held_sum, "blk", split_axis=3, concat_axis=0, tiled=True)
    part_max = lax.all_to_all(held_max, "blk", split_axis=3, concat_axis=0, tiled=True)
    part_total = lax.all_to_all(held_total, "blk", split_axis=3, concat_axis=0, tiled=True)
    row_max = jnp.max(part_max, axis=0)
    factor = jnp.exp(part_max - row_max[None])
    local_sum = jnp.sum(part_sum * factor[..., None], axis=0)
    local_total = jnp.sum(part_total * factor, axis=0)
    global_max = lax.pmax(row_max, "ctx")
    factor = jnp.exp(row_max - global_max)
    full_sum, full_total = lax.psum((local_sum * factor[..., None], local_total * factor), "ctx")
    maps = full_sum / full_total[..., None]
    attended = maps[:, 0] - lambdas[:, None, None] * maps[:, 1]
    spread = jnp.sqrt(jnp.mean(attended * attended, axis=-1, keepdims=True) + 1e-05)
    normed = attended / spread * gain.reshape(head_count, 1, value_dim)
    return normed.transpose(1, 0, 2).reshape(row_count, head_count * value_dim).astype(jnp.bfloat16)


def solution(mesh):
    return jax.shard_map(
        per_device,
        mesh=mesh,
        in_specs=(P("blk", None), P(("ctx", "blk"), None), P(("ctx", "blk"), None), P(), P(), P()),
        out_specs=P("blk", None),
        check_vma=False,
    )
```

profile of v0, /device:TPU:1, one launch (start us, length us, event | category | flops | bytes accessed | tf_op | source)
XLA Modules:
  0.0 702.6 jit_solution(5089112756356448077)
XLA Ops:
  7.2 4.2 reshape.41
  11.5 31.1 %all_gather.3 = bf16[128,2560]{1,0:T(8,128)(2,1)S(1)} all-gather(bf16[16,2560]{1,0:T(8,128)(2,1)S(1)} %copy-done.2), channel_id=1, replica_groups=mesh['ctx'=64,'blk'=8] {'blk'}, dimensions={0}, use_global_device_ids=true | all-gather | bytes 737280 | tf_op jit(solution)/shard_map/all_gather | solution.py:19
  42.5 0.3 copy.28
  43.0 1.2 fusion
  44.2 2.0 copy-done
  46.2 1.3 fusion.1
  47.6 0.1 copy.37
  47.7 0.8 reshape.46
  48.5 5.4 all-to-all-start.2
  54.0 0.1 copy.35
  54.1 0.8 reshape.44
  54.9 2.4 copy.31
  57.3 3.2 all-to-all-done.2
  60.5 3.5 all-to-all-start.1
  64.0 3.9 fusion.13
  67.9 3.5 copy.33
  71.4 6.8 all-to-all-start
  78.2 0.5 broadcast.28
  78.8 0.7 reduce.1
  79.4 0.2 reshape.47
  79.7 0.2 copy.38
  79.9 0.7 reduce.2
  80.5 0.2 reshape.45
  80.8 0.2 copy.36
  81.0 219.8 %pmax.7 = f32[10,2,16]{2,1,0:T(2,128)S(1)} all-reduce(f32[10,2,16]{2,1,0:T(2,128)S(1)} %bitcast_reduce_fusion), channel_id=1, replica_groups=mesh['ctx'=64,'blk'=8] {'ctx'}, use_global_device_ids=true, to_apply=%region_3.4 | all-reduce | flops 320 | bytes 2560 | tf_op jit(solution)/shard_map/pmax | solution.py:46
  300.9 0.5 fusion.3
  301.3 0.8 broadcast_multiply_fusion
  302.2 207.5 %psum.15 = f32[10,2,16]{2,1,0:T(2,128)S(1)} all-reduce(f32[10,2,16]{2,1,0:T(2,128)S(1)} %get-tuple-element.5), channel_id=1, replica_groups=mesh['ctx'=64,'blk'=8] {'ctx'}, use_global_device_ids=true, to_apply=%region_7.8 | all-reduce | flops 320 | bytes 2560 | tf_op jit(solution)/shard_map/psum | solution.py:48
  509.7 184.0 %all-reduce.2.cloned.1.call-done = f32[10,2,16,256]{3,2,1,0:T(8,128)} async-done(((f32[10,2,16,256]{3,2,1,0:T(8,128)}), f32[10,2,16,256]{3,2,1,0:T(8,128)}) %all-reduce.2.cloned.1.call-update) | async-done | bytes 327696 | tf_op jit(solution)/shard_map/psum | solution.py:48
  693.7 1.1 broadcast_divide_fusion
  694.8 0.2 multiply_reduce_fusion
  695.1 0.6 copy.46
  (22 shorter events, 0.4 us)
Async XLA Ops:
  6.5 4.9 copy-start.2
  44.2 2.0 copy-start
  44.2 10.7 %copy-start.1 = (bf16[384,2560]{1,0:T(8,128)(2,1)S(1)}, bf16[384,2560]{1,0:T(8,128)(2,1)}, u32[]{:S(2)}) copy-start(bf16[384,2560]{1,0:T(8,128)(2,1)} %param.8) | copy-start | bytes 5898244
  48.5 12.0 %all-to-all-start.2 = ((f32[8,1,320]{2,1,0:T(1,128)}), f32[8,1,320]{2,1,0:T(1,128)S(1)}, u32[]{:S(2)}, u32[]{:S(2)}) async-start(f32[8,1,320]{2,1,0:T(1,128)} %reshape.46), calls=%async_computation.2 | async-start | bytes 24576 | tf_op jit(solution)/shard_map/all_to_all | solution.py:41
  60.5 10.9 %all-to-all-start.1 = ((f32[8,1,320]{2,1,0:T(1,128)}), f32[8,1,320]{2,1,0:T(1,128)S(1)}, u32[]{:S(2)}, u32[]{:S(2)}) async-start(f32[8,1,320]{2,1,0:T(1,128)} %reshape.44), calls=%async_computation.1 | async-start | bytes 24576 | tf_op jit(solution)/shard_map/all_to_all | solution.py:40
  71.4 230.8 %copy-start.3 = (f32[2560]{0:T(1024)S(1)}, f32[2560]{0:T(1024)}, u32[]{:S(2)}) copy-start(f32[2560]{0:T(1024)} %param.11) | copy-start | bytes 30724
  71.4 229.4 %all-to-all-start = ((f32[1,10,2,128,256]{4,2,1,0,3:T(2,128)}), f32[1,10,2,128,256]{4,2,1,0,3:T(2,128)S(1)}, u32[]{:S(2)}, u32[]{:S(2)}) async-start(f32[1,10,2,128,256]{4,2,1,0,3:T(2,128)} %copy.33), calls=%async_computation | async-start | bytes 5242880 | tf_op jit(solution)/shard_map/all_to_all | solution.py:39
  78.2 616.6 %copy-start.4 = (f32[10]{0:T(128)S(1)}, f32[10]{0:T(128)}, u32[]{:S(2)}) copy-start(f32[10]{0:T(128)} %param.10) | copy-start | bytes 124
  78.2 615.5 %all-reduce.2.cloned.1.call-start = ((), (), s32[]{:S(2)}) async-start(), calls=%async_computation.3 | async-start | bytes 655360 | tf_op jit(solution)/shard_map/psum | solution.py:48
Sparse Core Ops, SparseCore 0:
  302.3 391.2 all-reduce.1
where the time goes:
time: 704 us; the launch traced here: 703 us
  blocking collectives  458 us (65%)
  waiting for transfers between devices  187 us (27%)
  local copies, waits for them, and re-layouts  16.3 us (2%)
  starting transfers between devices  15.7 us (2%)
  between operations  14.3 us (2%)
    pmax x1, blocking collectives, per_device(): global_max = lax.pmax(row_max, 'ctx')  220 us
    psum x1, blocking collectives, per_device(): lax.psum((local_sum * factor[..., None], local_total * factor), 'ctx')  207 us
    psum x1, waiting for transfers between devices, per_device(): lax.psum((local_sum * factor[..., None], local_total * factor), 'ctx')  184 us
    all_gather x1, blocking collectives, per_device(): query_rows = lax.all_gather(queries, 'blk', axis=0, tiled=True)  31.1 us
  transfers between devices with their start and end apart: 4, of which 2 were waited for; matrix products, arithmetic and copies ran while one was open for 2% of the time, Pallas kernels for 0%

commit v1 on v0

v1 whole, which is shorter than its diff:
```python
import functools
import math

import jax
import jax.numpy as jnp
from jax import lax
from jax.experimental import pallas as pl
from jax.experimental.pallas import tpu as pltpu
from jax.sharding import PartitionSpec as P

NX, NY, NZ = 4, 4, 16
CHUNK = 8
HEADS = 5
HALF_Z = NZ // 2
REACH = 3
DH = 128
WIDE = 2 * DH
KEYS = 384
HIDDEN = -1e30
MESH = pl.DeviceIdType.MESH


LAG = 2


def wrap(index, size):
    return jnp.where(index >= size, index - size, index)


def wait_bytes(ref, sem):
    pltpu.make_async_copy(ref, ref, sem).wait()


def send(src, dst, ssem, rsem, to):
    copy = pltpu.make_async_remote_copy(
        src_ref=src, dst_ref=dst, send_sem=ssem, recv_sem=rsem, device_id=to, device_id_type=MESH
    )
    copy.start()
    return copy


def loop(count, body, start=0):
    def step(i, carry):
        body(i)
        return carry

    lax.fori_loop(start, count, step, 0)


def merge_rows(rows):
    top = functools.reduce(jnp.maximum, rows)
    parts = [jnp.exp2(row - top) for row in rows]
    total = functools.reduce(jnp.add, parts)
    inverse = 1.0 / total
    return [part * inverse for part in parts], top + jnp.log2(total)


def column(row):
    lead = row.shape[:-2]
    lane = lax.broadcasted_iota(jnp.int32, lead + (16, 128), len(lead) + 1)
    sub = lax.broadcasted_iota(jnp.int32, lead + (16, 128), len(lead))
    wide = jnp.where(lane == sub, jnp.broadcast_to(row, lead + (16, 128)), 0.0)
    return jnp.sum(wide, axis=-1, keepdims=True)


def weighted(weights, parts):
    acc = None
    for weight, part in zip(weights, parts):
        term = column(weight) * part.astype(jnp.float32)
        acc = term if acc is None else acc + term
    return acc


def kernel(
    offset_hbm, lam_hbm, gain_hbm, q_ref, k_ref, v_ref, out_ref,
    offset_ref, lam_ref, gain_ref,
    kbuf, vbuf, qbuf, bias, obuf, sbuf, part_a, part_b, srow_a, srow_b,
    send_a, send_b, srow2_a, srow2_b, got_a, got_b, sgot_a, sgot_b,
    zsend, zsrow, zbuf, zsbuf, fin,
    small_sem, kl_sem, vl_sem, ql_sem, k_ssem, k_rsem, v_ssem, v_rsem, q_ssem, q_rsem,
    a_ssem, a_rsem, b_ssem, b_rsem, ta_ssem, ta_rsem, tb_ssem, tb_rsem,
    a2_ssem, a2_rsem, b2_ssem, b2_rsem, ta2_ssem, ta2_rsem, tb2_ssem, tb2_rsem,
    z_ssem, z_rsem, zt_ssem, zt_rsem, g_ssem, g_rsem, token_sem,
):
    ctx = lax.axis_index("ctx")
    blk = lax.axis_index("blk")
    core = lax.rem(ctx, 2)
    z = lax.rem(ctx // 2, NZ)
    y_lo = ctx // (2 * NZ)
    x = blk // 2
    y = lax.rem(blk, 2) * 2 + y_lo
    other = 1 - core
    y_hi = lax.rem(blk, 2)
    xs = [wrap(x + d, NX) for d in range(1, NX)]
    ys = [wrap(y + d, NY) for d in range(1, NY)]
    beside = (ctx + other - core, blk)
    pair = (ctx + 2 * NZ * (1 - 2 * y_lo), blk)
    x_line = [(ctx, xx * 2 + y_hi) for xx in xs]
    y_line = [((lax.rem(yy, 2) * NZ + z) * 2 + core, x * 2 + yy // 2) for yy in ys]
    mirror = [(pair[0], xx * 2 + 1 - y_hi) for xx in [x] + xs]
    z_base = y_lo * 2 * NZ + core

    def z_line(d):
        return (z_base + 2 * wrap(z + d, NZ), blk)

    steps = (0, other - core, 2 * NZ * (1 - 2 * y_lo), 2 * NZ * (1 - 2 * y_lo) + other - core)

    def column_at(i, zz):
        return (z_base + steps[i] + 2 * zz, blk)

    def cols(which, head, count=1):
        return pl.ds(pl.multiple_of(which * (HEADS * WIDE) + head * WIDE, WIDE), count * WIDE)

    barrier = pltpu.get_barrier_semaphore()

    def greet(to):
        pl.semaphore_signal(barrier, inc=1, device_id=to, device_id_type=MESH)

    near = [beside] + x_line + y_line + mirror[1:] + [z_line(1), z_line(NZ - 1), column_at(3, z)]
    for to in near:
        greet(to)

    def own_copies(h):
        return (
            pltpu.make_async_copy(k_ref.at[:, cols(core, h)], kbuf.at[0, h], kl_sem.at[h]),
            pltpu.make_async_copy(v_ref.at[:, cols(core, h)], vbuf.at[0, h], vl_sem.at[h]),
        )

    def start_own(h):
        for copy in own_copies(h):
            copy.start()

    own_q = pltpu.make_async_copy(q_ref.at[:, cols(core, 0, HEADS)], qbuf.at[blk], ql_sem)
    own_q.start()
    loop(HEADS, start_own)
    small = [
        pltpu.make_async_copy(offset_hbm, offset_ref, small_sem.at[0]),
        pltpu.make_async_copy(lam_hbm, lam_ref, small_sem.at[1]),
        pltpu.make_async_copy(gain_hbm, gain_ref, small_sem.at[2]),
    ]
    for copy in small:
        copy.start()
    pl.semaphore_wait(barrier, len(near))

    def pushes(h):
        return (
            pltpu.make_async_remote_copy(
                src_ref=k_ref.at[:, cols(other, h)], dst_ref=kbuf.at[1, h], send_sem=k_ssem.at[h],
                recv_sem=k_rsem.at[h], device_id=beside, device_id_type=MESH,
            ),
            pltpu.make_async_remote_copy(
                src_ref=v_ref.at[:, cols(other, h)], dst_ref=vbuf.at[1, h], send_sem=v_ssem.at[h],
                recv_sem=v_rsem.at[h], device_id=beside, device_id_type=MESH,
            ),
        )

    def push(h):
        for copy in pushes(h):
            copy.start()

    def queries_of(h):
        return qbuf.at[pl.ds(0, 7), :, cols(0, h)]

    def push_head(h):
        mine = q_ref.at[:, cols(core, h)]
        for to in mirror + x_line:
            send(mine, qbuf.at[blk, :, cols(0, h)], q_ssem.at[h], q_rsem.at[h], to)
        push(h)

    loop(HEADS, push_head)

    def token(step):
        for d in (2**step, NZ - 2**step):
            pl.semaphore_signal(token_sem.at[step], inc=1, device_id=z_line(d), device_id_type=MESH)

    token(0)

    row = lax.broadcasted_iota(jnp.int32, (32 * CHUNK, KEYS), 0)
    pos = lax.broadcasted_iota(jnp.int32, (32 * CHUNK, KEYS), 1)
    ahead = pos - (lax.shift_right_logical(row, 4) * CHUNK + (row & (CHUNK - 1)))
    small[0].wait()
    for s in range(2):
        owner = ctx if s == 0 else ctx + other - core
        start = (owner * 8 + blk) * KEYS
        bias[s] = jnp.where(ahead <= offset_ref[0] - start, 0.0, HIDDEN)

    scale = DH ** (-0.5) * math.log2(math.e)

    def attend(h):
        own_k, own_v = own_copies(h)
        wait_bytes(queries_of(h), q_rsem.at[h])
        own_k.wait()
        wait_bytes(kbuf.at[1, h], k_rsem.at[h])
        lane3 = lax.broadcasted_iota(jnp.int32, (16, CHUNK, WIDE), 2)
        q = qbuf[:, :, cols(0, h)].astype(jnp.float32).reshape(16, CHUNK, WIDE)
        low = jnp.where(lane3 < DH, q, 0.0)
        high = jnp.where(lane3 >= DH, q, 0.0)
        both = jnp.concatenate([low, high], axis=1).reshape(256, WIDE).astype(jnp.bfloat16)
        scores = []
        for s in range(2):
            dot = lax.dot_general(
                both, kbuf[s, h], (((1,), (1,)), ((), ())), preferred_element_type=jnp.float32
            )
            scores.append(dot * scale + bias[s])
        top = jnp.max(jnp.maximum(scores[0], scores[1]), axis=1, keepdims=True)
        expo = [jnp.exp2(t - top) for t in scores]
        total = jnp.sum(expo[0] + expo[1], axis=1, keepdims=True)
        own_v.wait()
        wait_bytes(vbuf.at[1, h], v_rsem.at[h])
        out = sum(
            jnp.dot(expo[s].astype(jnp.bfloat16), vbuf[s, h], preferred_element_type=jnp.float32)
            for s in range(2)
        )
        out = (out * (1.0 / total)).reshape(NX, NY, 16, WIDE).astype(jnp.bfloat16)
        obuf[h, 0] = out[..., :DH]
        obuf[h, 1] = out[..., DH:]
        stat_lane = lax.broadcasted_iota(jnp.int32, (16, 16, 128), 2)
        stat_sub = lax.broadcasted_iota(jnp.int32, (16, 16, 128), 1)
        stat = jnp.broadcast_to((top + jnp.log2(total)).reshape(16, 16, 1), (16, 16, 128))
        spread = jnp.where(stat_lane == stat_sub, stat, 0.0)
        sbuf[h] = jnp.sum(spread, axis=1, keepdims=True).reshape(NX, NY, 1, 128)
        for d in range(NX - 1):
            send(sbuf.at[h, xs[d]], srow_a.at[h, d], ta_ssem.at[h], ta_rsem.at[h], x_line[d])
            send(sbuf.at[h, :, ys[d]], srow_b.at[h, d], tb_ssem.at[h], tb_rsem.at[h], y_line[d])
        for d in range(NX - 1):
            send(obuf.at[h, 0, xs[d]], part_a.at[h, d], a_ssem.at[h], a_rsem.at[h], x_line[d])
            send(obuf.at[h, 1, :, ys[d]], part_b.at[h, d], b_ssem.at[h], b_rsem.at[h], y_line[d])

    def first_step(h):
        wait_bytes(srow_a.at[h], ta_rsem.at[h])
        weights_a, whole_a = merge_rows([sbuf[h, x]] + [srow_a[h, d] for d in range(NX - 1)])
        srow2_a[h] = whole_a
        wait_bytes(srow_b.at[h], tb_rsem.at[h])
        weights_b, whole_b = merge_rows([sbuf[h, :, y]] + [srow_b[h, d] for d in range(NY - 1)])
        srow2_b[h] = whole_b
        for d in range(NX - 1):
            send(srow2_a.at[h, ys[d]], sgot_a.at[h, d], ta2_ssem.at[h], ta2_rsem.at[h], y_line[d])
            send(srow2_b.at[h, xs[d]], sgot_b.at[h, d], tb2_ssem.at[h], tb2_rsem.at[h], x_line[d])
        wait_bytes(part_a.at[h], a_rsem.at[h])
        parts = [obuf[h, 0, x]] + [part_a[h, d] for d in range(NX - 1)]
        send_a[h] = weighted(weights_a, parts).astype(jnp.bfloat16)
        wait_bytes(part_b.at[h], b_rsem.at[h])
        parts = [obuf[h, 1, :, y]] + [part_b[h, d] for d in range(NY - 1)]
        send_b[h] = weighted(weights_b, parts).astype(jnp.bfloat16)
        for d in range(NX - 1):
            send(send_a.at[h, ys[d]], got_a.at[h, d], a2_ssem.at[h], a2_rsem.at[h], y_line[d])
            send(send_b.at[h, xs[d]], got_b.at[h, d], b2_ssem.at[h], b2_rsem.at[h], x_line[d])

    def owner_of(h):
        return lax.rem(3 * h + HALF_Z - core, HALF_Z)

    def second_step(h):
        wait_bytes(sgot_a.at[h], ta2_rsem.at[h])
        wait_bytes(sgot_b.at[h], tb2_rsem.at[h])
        weights_a, whole_a = merge_rows([srow2_a[h, y]] + [sgot_a[h, d] for d in range(NY - 1)])
        weights_b, _ = merge_rows([srow2_b[h, x]] + [sgot_b[h, d] for d in range(NX - 1)])
        zsrow[h] = whole_a
        wait_bytes(got_a.at[h], a2_rsem.at[h])
        parts = [send_a[h, y]] + [got_a[h, d] for d in range(NY - 1)]
        zsend[h, :, :DH] = weighted(weights_a, parts).astype(jnp.bfloat16)
        wait_bytes(got_b.at[h], b2_rsem.at[h])
        parts = [send_b[h, x]] + [got_b[h, d] for d in range(NX - 1)]
        zsend[h, :, DH:] = weighted(weights_b, parts).astype(jnp.bfloat16)
        for i in range(2):
            owner = owner_of(h) + i * HALF_Z
            gap = wrap(owner - z + NZ, NZ)

            @pl.when(gap != 0)
            def _():
                to = (z_base + 2 * owner, blk)
                send(zsrow.at[h], zsbuf.at[gap - 1], zt_ssem.at[h, i], zt_rsem, to)
                send(zsend.at[h], zbuf.at[gap - 1], z_ssem.at[h, i], z_rsem, to)

    def turn_of(i):
        @pl.when(i < HEADS)
        def _():
            attend(i)

        for step in range(2):

            @pl.when(i == LAG + step)
            def _():
                pl.semaphore_wait(token_sem.at[step], 2)
                token(step + 1)

        @pl.when(i == 2 * LAG)
        def _():
            pl.semaphore_wait(token_sem.at[2], 2)

        @pl.when(jnp.logical_and(i >= LAG, i < HEADS + LAG))
        def _():
            first_step(i - LAG)

        @pl.when(i >= 2 * LAG)
        def _():
            second_step(i - 2 * LAG)

    own_q.wait()
    loop(HEADS + 2 * LAG, turn_of)

    mine = lax.rem(3 * (z + core), HALF_Z)
    is_owner = mine < HEADS
    all_tiles = 4 * HEADS
    small[1].wait()
    small[2].wait()

    @pl.when(is_owner)
    def _():
        wait_bytes(zsbuf, zt_rsem)
        weights, _ = merge_rows([zsrow[mine]] + [zsbuf[d] for d in range(NZ - 1)])
        wait_bytes(zbuf, z_rsem)
        acc = weighted(weights, [zsend[mine]] + [zbuf[d] for d in range(NZ - 1)])
        head = core * HEADS + mine
        attended = acc[:CHUNK] - lam_ref[head] * acc[CHUNK:]
        spread = jnp.sqrt(jnp.mean(attended * attended, axis=-1, keepdims=True) + 1e-5)
        normed = attended / spread * gain_ref[cols(0, head)].reshape(1, WIDE)
        halves = jnp.concatenate([normed[:, :DH], normed[:, DH:]], axis=0)
        slot = (y_lo * 2 + core) * HEADS + mine
        fin[slot] = halves.astype(jnp.bfloat16)
        tile = fin.at[slot]

        def give(d):
            zz = wrap(wrap(z + d + NZ - REACH, 2 * NZ), NZ)
            for i in range(1, 4):
                send(tile, tile, g_ssem.at[i], g_rsem, column_at(i, zz))

            @pl.when(zz != z)
            def _():
                send(tile, tile, g_ssem.at[0], g_rsem, column_at(0, zz))

        loop(HALF_Z, give)
        wait_bytes(fin.at[pl.ds(0, all_tiles - 1)], g_rsem)

    @pl.when(jnp.logical_not(is_owner))
    def _():
        wait_bytes(fin, g_rsem)

    def assemble(h):
        for c in range(2):
            first = fin[c * HEADS + h].astype(jnp.float32)
            second = fin[(2 + c) * HEADS + h].astype(jnp.float32)
            low = jnp.concatenate([first[:CHUNK], second[:CHUNK]], axis=0)
            high = jnp.concatenate([first[CHUNK:], second[CHUNK:]], axis=0)
            out_ref[:, cols(c, h)] = jnp.concatenate([low, high], axis=1).astype(jnp.bfloat16)

    loop(HEADS, assemble)

    def left(h):
        for copy in pushes(h):
            copy.wait_send()
        wait_bytes(queries_of(h), q_ssem.at[h])
        for part, sem in (
            (part_a, a_ssem), (part_b, b_ssem), (srow_a, ta_ssem), (srow_b, tb_ssem),
            (got_a, a2_ssem), (got_b, b2_ssem), (sgot_a, ta2_ssem), (sgot_b, tb2_ssem),
        ):
            wait_bytes(part.at[h], sem.at[h])

        for i in range(2):

            @pl.when(owner_of(h) + i * HALF_Z != z)
            def _():
                wait_bytes(zsend.at[h], z_ssem.at[h, i])
                wait_bytes(zsrow.at[h], zt_ssem.at[h, i])

    loop(HEADS, left)
    @pl.when(is_owner)
    def _():
        wait_bytes(fin.at[pl.ds(0, HALF_Z - 1)], g_ssem.at[0])
        for i in range(1, 4):
            wait_bytes(fin.at[pl.ds(0, HALF_Z)], g_ssem.at[i])


def per_device(queries, keys, values, offset, lambdas, gain):
    row_count, width = queries.shape
    bf16, f32 = jnp.bfloat16, jnp.float32
    dma = pltpu.SemaphoreType.DMA
    heads = dma((HEADS,))
    hbm = pl.BlockSpec(memory_space=pltpu.HBM)
    vmem = pl.BlockSpec(memory_space=pltpu.VMEM)
    return pl.pallas_call(
        kernel,
        out_shape=jax.ShapeDtypeStruct((row_count, width), bf16),
        in_specs=[hbm] * 6,
        out_specs=vmem,
        scratch_shapes=[
            pltpu.SMEM((1,), jnp.int32),
            pltpu.SMEM(lambdas.shape, f32),
            pltpu.VMEM(gain.shape, f32),
            pltpu.VMEM((2, HEADS, KEYS, WIDE), bf16),
            pltpu.VMEM((2, HEADS, KEYS, WIDE), bf16),
            pltpu.VMEM((8, 16, HEADS * WIDE), bf16),
            pltpu.VMEM((2, 256, KEYS), f32),
            pltpu.VMEM((HEADS, 2, NX, NY, 16, DH), bf16),
            pltpu.VMEM((HEADS, NX, NY, 1, 128), f32),
            pltpu.VMEM((HEADS, NX - 1, NY, 16, DH), bf16),
            pltpu.VMEM((HEADS, NY - 1, NX, 16, DH), bf16),
            pltpu.VMEM((HEADS, NX - 1, NY, 1, 128), f32),
            pltpu.VMEM((HEADS, NY - 1, NX, 1, 128), f32),
            pltpu.VMEM((HEADS, NY, 16, DH), bf16),
            pltpu.VMEM((HEADS, NX, 16, DH), bf16),
            pltpu.VMEM((HEADS, NY, 1, 128), f32),
            pltpu.VMEM((HEADS, NX, 1, 128), f32),
            pltpu.VMEM((HEADS, NY - 1, 16, DH), bf16),
            pltpu.VMEM((HEADS, NX - 1, 16, DH), bf16),
            pltpu.VMEM((HEADS, NY - 1, 1, 128), f32),
            pltpu.VMEM((HEADS, NX - 1, 1, 128), f32),
            pltpu.VMEM((HEADS, 16, WIDE), bf16),
            pltpu.VMEM((HEADS, 1, 128), f32),
            pltpu.VMEM((NZ - 1, 16, WIDE), bf16),
            pltpu.VMEM((NZ - 1, 1, 128), f32),
            pltpu.VMEM((4 * HEADS, 16, DH), bf16),
            dma((3,)), heads, heads, dma,
            heads, heads, heads, heads, heads, heads,
            heads, heads, heads, heads, heads, heads, heads, heads,
            heads, heads, heads, heads, heads, heads, heads, heads,
            dma((HEADS, 2)), dma, dma((HEADS, 2)), dma, dma((4,)), dma,
            pltpu.SemaphoreType.REGULAR((3,)),
        ],
        compiler_params=pltpu.CompilerParams(
            collective_id=0, has_side_effects=True, vmem_limit_bytes=64 * 1024 * 1024
        ),
        cost_estimate=pl.CostEstimate(flops=800_000_000, bytes_accessed=8_000_000, transcendentals=1_000_000),
    )(offset, lambdas, gain, queries, keys, values)


def solution(mesh):
    return jax.shard_map(
        per_device,
        mesh=mesh,
        in_specs=(P("blk", None), P(("ctx", "blk"), None), P(("ctx", "blk"), None), P(), P(), P()),
        out_specs=P("blk", None),
        check_vma=False,
    )
```

time: 704 us -> 52.3 us (0.07)
  blocking collectives: 458 us -> 0 us
  waiting for transfers between devices: 187 us -> 0 us
  Pallas kernels: 0 us -> 50 us
  starting transfers between devices: 15.7 us -> 0 us
  local copies, waits for them, and re-layouts: 16.3 us -> 1.53 us
  between operations: 14.3 us -> 0.66 us
    pmax x1 -> x0, blocking collectives: 220 us -> none  [per_device(): global_max = lax.pmax(row_max, 'ctx')]
    psum x1 -> x0, blocking collectives: 207 us -> none  [per_device(): lax.psum((local_sum * factor[..., None], local_total * factor), 'ctx')]
    psum x1 -> x0, waiting for transfers between devices: 184 us -> none  [per_device(): lax.psum((local_sum * factor[..., None], local_total * factor), 'ctx')]
    pallas_call x0 -> x1, Pallas kernels: none -> 50 us  [per_device(): pl.pallas_call(kernel, out_shape=jax.ShapeDtypeStruct((row_count, width),...]
    all_gather x1 -> x0, blocking collectives: 31.1 us -> none  [per_device(): query_rows = lax.all_gather(queries, 'blk', axis=0, tiled=True)]
    all_to_all x3 -> x0, starting transfers between devices: 15.7 us -> none  [the longest x1 6.78 us: per_device(): lax.all_to_all(held_sum, 'blk', split_axis=3, concat_axis=0, tiled=True)]
  transfers between devices with their start and end apart: 4 -> 0, of which waited for: 2 -> 0; matrix products, arithmetic and copies ran while one was open for 2% -> 0% of each run, Pallas kernels for 0% -> 0%
where the time goes in v1:
time: 52.3 us; the launch traced here: 52.2 us
  Pallas kernels  50 us (96%)
  local copies, waits for them, and re-layouts  1.53 us (3%)
  between operations  0.66 us (1%)
    pallas_call x1, Pallas kernels, per_device(): pl.pallas_call(kernel, out_shape=jax.ShapeDtypeStruct((row_count, width),...  50 us
    unnamed x1, local copies, waits for them, and re-layouts  1.53 us

profile of v1, /device:TPU:1, one launch (start us, length us, event | category | flops | bytes accessed | tf_op | source)
XLA Modules:
  0.0 52.2 jit_solution(14755112623688529645)
XLA Ops:
  0.7 50.0 %shard_map.64 = bf16[16,2560]{1,0:T(8,128)(2,1)} custom-call(s32[1]{0:T(128)S(6)} %copy.8.offset_hbm, f32[10]{0:T(128)} %lam_hbm.1, f32[2560]{0:T(1024)} %gain_hbm.1, bf16[16,2560]{1,0:T(8,128)(2,1)} %q_ref.1, bf16[384,2560]{1,0:T(8,128)(2,1)} %k_ref.1, bf16[384,2560]{1,0:T(8,128)(2,1)} %v_ref.1), custom_call_target="tpu_custom_call" | custom-call | flops 800000000 | bytes 8000000 | tf_op jit(solution)/shard_map/pallas_call | solution.py:380
  50.7 1.5 %copy.9 = bf16[16,2560]{1,0:T(8,128)(2,1)} copy(bf16[16,2560]{1,0:T(8,128)(2,1)} %shard_map.64) | data formatting | bytes 163840

commit v2 on v1

--- a/solution.py
+++ b/solution.py
@@ -74,7 +74,7 @@
 def kernel(
     offset_hbm, lam_hbm, gain_hbm, q_ref, k_ref, v_ref, out_ref,
     offset_ref, lam_ref, gain_ref,
-    kbuf, vbuf, qbuf, bias, obuf, sbuf, part_a, part_b, srow_a, srow_b,
+    kbuf, vbuf, qbuf, bias, tall, scores, expo, inverse, maps, obuf, sbuf, part_a, part_b, srow_a, srow_b,
     send_a, send_b, srow2_a, srow2_b, got_a, got_b, sgot_a, sgot_b,
     zsend, zsrow, zbuf, zsbuf, fin,
     small_sem, kl_sem, vl_sem, ql_sem, k_ssem, k_rsem, v_ssem, v_rsem, q_ssem, q_rsem,
@@ -122,8 +122,8 @@
 
     def own_copies(h):
         return (
-            pltpu.make_async_copy(k_ref.at[:, cols(core, h)], kbuf.at[0, h], kl_sem.at[h]),
-            pltpu.make_async_copy(v_ref.at[:, cols(core, h)], vbuf.at[0, h], vl_sem.at[h]),
+            pltpu.make_async_copy(k_ref.at[:, cols(core, h)], kbuf.at[h, pl.ds(0, KEYS)], kl_sem.at[h]),
+            pltpu.make_async_copy(v_ref.at[:, cols(core, h)], vbuf.at[h, pl.ds(0, KEYS)], vl_sem.at[h]),
         )
 
     def start_own(h):
@@ -145,11 +145,11 @@
     def pushes(h):
         return (
             pltpu.make_async_remote_copy(
-                src_ref=k_ref.at[:, cols(other, h)], dst_ref=kbuf.at[1, h], send_sem=k_ssem.at[h],
+                src_ref=k_ref.at[:, cols(other, h)], dst_ref=kbuf.at[h, pl.ds(KEYS, KEYS)], send_sem=k_ssem.at[h],
                 recv_sem=k_rsem.at[h], device_id=beside, device_id_type=MESH,
             ),
             pltpu.make_async_remote_copy(
-                src_ref=v_ref.at[:, cols(other, h)], dst_ref=vbuf.at[1, h], send_sem=v_ssem.at[h],
+                src_ref=v_ref.at[:, cols(other, h)], dst_ref=vbuf.at[h, pl.ds(KEYS, KEYS)], send_sem=v_ssem.at[h],
                 recv_sem=v_rsem.at[h], device_id=beside, device_id_type=MESH,
             ),
         )
@@ -182,43 +182,44 @@
     for s in range(2):
         owner = ctx if s == 0 else ctx + other - core
         start = (owner * 8 + blk) * KEYS
-        bias[s] = jnp.where(ahead <= offset_ref[0] - start, 0.0, HIDDEN)
+        bias[:, s * KEYS : s * KEYS + KEYS] = jnp.where(ahead <= offset_ref[0] - start, 0.0, HIDDEN)
 
     scale = DH ** (-0.5) * math.log2(math.e)
 
     def attend(h):
         own_k, own_v = own_copies(h)
         wait_bytes(queries_of(h), q_rsem.at[h])
+        blocks = [slice(32 * b, 32 * b + 32) for b in range(8)]
+        lane = lax.broadcasted_iota(jnp.int32, (2, CHUNK, WIDE), 2)
+        for b, rows in enumerate(blocks):
+            q = qbuf[b, :, cols(0, h)].astype(jnp.float32).reshape(2, CHUNK, WIDE)
+            both = jnp.concatenate([jnp.where(lane < DH, q, 0.0), jnp.where(lane >= DH, q, 0.0)], axis=1)
+            tall[rows] = both.reshape(32, WIDE).astype(jnp.bfloat16)
         own_k.wait()
-        wait_bytes(kbuf.at[1, h], k_rsem.at[h])
-        lane3 = lax.broadcasted_iota(jnp.int32, (16, CHUNK, WIDE), 2)
-        q = qbuf[:, :, cols(0, h)].astype(jnp.float32).reshape(16, CHUNK, WIDE)
-        low = jnp.where(lane3 < DH, q, 0.0)
-        high = jnp.where(lane3 >= DH, q, 0.0)
-        both = jnp.concatenate([low, high], axis=1).reshape(256, WIDE).astype(jnp.bfloat16)
-        scores = []
-        for s in range(2):
-            dot = lax.dot_general(
-                both, kbuf[s, h], (((1,), (1,)), ((), ())), preferred_element_type=jnp.float32
-            )
-            scores.append(dot * scale + bias[s])
-        top = jnp.max(jnp.maximum(scores[0], scores[1]), axis=1, keepdims=True)
-        expo = [jnp.exp2(t - top) for t in scores]
-        total = jnp.sum(expo[0] + expo[1], axis=1, keepdims=True)
+        wait_bytes(kbuf.at[h, pl.ds(KEYS, KEYS)], k_rsem.at[h])
+        scores[...] = lax.dot_general(
+            tall[...], kbuf[h], (((1,), (1,)), ((), ())), preferred_element_type=jnp.float32
+        )
+        stat_lane = lax.broadcasted_iota(jnp.int32, (2, 16, 128), 2)
+        stat_sub = lax.broadcasted_iota(jnp.int32, (2, 16, 128), 1)
+        for b, rows in enumerate(blocks):
+            score = scores[rows] * scale + bias[rows]
+            top = jnp.max(score, axis=1, keepdims=True)
+            e = jnp.exp2(score - top)
+            total = jnp.sum(e, axis=1, keepdims=True)
+            expo[rows] = e.astype(jnp.bfloat16)
+            inverse[rows] = jnp.broadcast_to(1.0 / total, (32, 128))
+            stat = jnp.broadcast_to((top + jnp.log2(total)).reshape(2, 16, 1), (2, 16, 128))
+            stat = jnp.where(stat_lane == stat_sub, stat, 0.0)
+            sbuf[h, b // 2, (b % 2) * 2 : (b % 2) * 2 + 2] = jnp.sum(stat, axis=1, keepdims=True)
         own_v.wait()
-        wait_bytes(vbuf.at[1, h], v_rsem.at[h])
-        out = sum(
-            jnp.dot(expo[s].astype(jnp.bfloat16), vbuf[s, h], preferred_element_type=jnp.float32)
-            for s in range(2)
-        )
-        out = (out * (1.0 / total)).reshape(NX, NY, 16, WIDE).astype(jnp.bfloat16)
-        obuf[h, 0] = out[..., :DH]
-        obuf[h, 1] = out[..., DH:]
-        stat_lane = lax.broadcasted_iota(jnp.int32, (16, 16, 128), 2)
-        stat_sub = lax.broadcasted_iota(jnp.int32, (16, 16, 128), 1)
-        stat = jnp.broadcast_to((top + jnp.log2(total)).reshape(16, 16, 1), (16, 16, 128))
-        spread = jnp.where(stat_lane == stat_sub, stat, 0.0)
-        sbuf[h] = jnp.sum(spread, axis=1, keepdims=True).reshape(NX, NY, 1, 128)
+        wait_bytes(vbuf.at[h, pl.ds(KEYS, KEYS)], v_rsem.at[h])
+        maps[...] = jnp.dot(expo[...], vbuf[h], preferred_element_type=jnp.float32)
+        for b, rows in enumerate(blocks):
+            for half in range(2):
+                part = maps[rows, half * DH : half * DH + DH] * inverse[rows]
+                part = part.reshape(2, 16, DH).astype(jnp.bfloat16)
+                obuf[h, half, b // 2, (b % 2) * 2 : (b % 2) * 2 + 2] = part
         for d in range(NX - 1):
             send(sbuf.at[h, xs[d]], srow_a.at[h, d], ta_ssem.at[h], ta_rsem.at[h], x_line[d])
             send(sbuf.at[h, :, ys[d]], srow_b.at[h, d], tb_ssem.at[h], tb_rsem.at[h], y_line[d])
@@ -386,10 +387,15 @@
             pltpu.SMEM((1,), jnp.int32),
             pltpu.SMEM(lambdas.shape, f32),
             pltpu.VMEM(gain.shape, f32),
-            pltpu.VMEM((2, HEADS, KEYS, WIDE), bf16),
-            pltpu.VMEM((2, HEADS, KEYS, WIDE), bf16),
+            pltpu.VMEM((HEADS, 2 * KEYS, WIDE), bf16),
+            pltpu.VMEM((HEADS, 2 * KEYS, WIDE), bf16),
             pltpu.VMEM((8, 16, HEADS * WIDE), bf16),
-            pltpu.VMEM((2, 256, KEYS), f32),
+            pltpu.VMEM((256, 2 * KEYS), f32),
+            pltpu.VMEM((256, WIDE), bf16),
+            pltpu.VMEM((256, 2 * KEYS), f32),
+            pltpu.VMEM((256, 2 * KEYS), bf16),
+            pltpu.VMEM((256, 128), f32),
+            pltpu.VMEM((256, WIDE), f32),
             pltpu.VMEM((HEADS, 2, NX, NY, 16, DH), bf16),
             pltpu.VMEM((HEADS, NX, NY, 1, 128), f32),
             pltpu.VMEM((HEADS, NX - 1, NY, 16, DH), bf16),

time: 52.3 us -> 52.3 us (level)
  no operation moved by 1% of the time
where the time goes in v2:
time: 52.3 us; the launch traced here: 52.2 us
  Pallas kernels  50 us (96%)
  local copies, waits for them, and re-layouts  1.53 us (3%)
  between operations  0.66 us (1%)
    pallas_call x1, Pallas kernels, per_device(): pl.pallas_call(kernel, out_shape=jax.ShapeDtypeStruct((row_count, width),...  50 us
    unnamed x1, local copies, waits for them, and re-layouts  1.53 us

profile of v2, /device:TPU:1, one launch (start us, length us, event | category | flops | bytes accessed | tf_op | source)
XLA Modules:
  0.0 52.2 jit_solution(7165862772201603821)
XLA Ops:
  0.7 50.0 %shard_map.64 = bf16[16,2560]{1,0:T(8,128)(2,1)} custom-call(s32[1]{0:T(128)S(6)} %copy.8.offset_hbm, f32[10]{0:T(128)} %lam_hbm.1, f32[2560]{0:T(1024)} %gain_hbm.1, bf16[16,2560]{1,0:T(8,128)(2,1)} %q_ref.1, bf16[384,2560]{1,0:T(8,128)(2,1)} %k_ref.1, bf16[384,2560]{1,0:T(8,128)(2,1)} %v_ref.1), custom_call_target="tpu_custom_call" | custom-call | flops 800000000 | bytes 8000000 | tf_op jit(solution)/shard_map/pallas_call | solution.py:381
  50.7 1.5 %copy.9 = bf16[16,2560]{1,0:T(8,128)(2,1)} copy(bf16[16,2560]{1,0:T(8,128)(2,1)} %shard_map.64) | data formatting | bytes 163840

commit v3 on v2

--- a/solution.py
+++ b/solution.py
@@ -74,12 +74,10 @@
 def kernel(
     offset_hbm, lam_hbm, gain_hbm, q_ref, k_ref, v_ref, out_ref,
     offset_ref, lam_ref, gain_ref,
-    kbuf, vbuf, qbuf, bias, tall, scores, expo, inverse, maps, obuf, sbuf, part_a, part_b, srow_a, srow_b,
-    send_a, send_b, srow2_a, srow2_b, got_a, got_b, sgot_a, sgot_b,
+    kbuf, vbuf, qbuf, bias, tall, scores, expo, inverse, maps, obuf, sbuf, part, part_row,
     zsend, zsrow, zbuf, zsbuf, fin,
     small_sem, kl_sem, vl_sem, ql_sem, k_ssem, k_rsem, v_ssem, v_rsem, q_ssem, q_rsem,
-    a_ssem, a_rsem, b_ssem, b_rsem, ta_ssem, ta_rsem, tb_ssem, tb_rsem,
-    a2_ssem, a2_rsem, b2_ssem, b2_rsem, ta2_ssem, ta2_rsem, tb2_ssem, tb2_rsem,
+    p_ssem, p_rsem, pr_ssem, pr_rsem,
     z_ssem, z_rsem, zt_ssem, zt_rsem, g_ssem, g_rsem, token_sem,
 ):
     ctx = lax.axis_index("ctx")
@@ -95,8 +93,14 @@
     ys = [wrap(y + d, NY) for d in range(1, NY)]
     beside = (ctx + other - core, blk)
     pair = (ctx + 2 * NZ * (1 - 2 * y_lo), blk)
+    ctx_of = [(lax.rem(yy, 2) * NZ + z) * 2 + core for yy in [y] + ys]
+    hi_of = [yy // 2 for yy in [y] + ys]
+    plane = [
+        (xx, yy, (ctx_of[j], xx * 2 + hi_of[j]))
+        for xx in [x] + xs
+        for j, yy in enumerate([y] + ys)
+    ][1:]
     x_line = [(ctx, xx * 2 + y_hi) for xx in xs]
-    y_line = [((lax.rem(yy, 2) * NZ + z) * 2 + core, x * 2 + yy // 2) for yy in ys]
     mirror = [(pair[0], xx * 2 + 1 - y_hi) for xx in [x] + xs]
     z_base = y_lo * 2 * NZ + core
 
@@ -116,7 +120,7 @@
     def greet(to):
         pl.semaphore_signal(barrier, inc=1, device_id=to, device_id_type=MESH)
 
-    near = [beside] + x_line + y_line + mirror[1:] + [z_line(1), z_line(NZ - 1), column_at(3, z)]
+    near = [beside] + [to for _, _, to in plane] + [z_line(1), z_line(NZ - 1), column_at(3, z)]
     for to in near:
         greet(to)
 
@@ -217,51 +221,24 @@
         maps[...] = jnp.dot(expo[...], vbuf[h], preferred_element_type=jnp.float32)
         for b, rows in enumerate(blocks):
             for half in range(2):
-                part = maps[rows, half * DH : half * DH + DH] * inverse[rows]
-                part = part.reshape(2, 16, DH).astype(jnp.bfloat16)
-                obuf[h, half, b // 2, (b % 2) * 2 : (b % 2) * 2 + 2] = part
-        for d in range(NX - 1):
-            send(sbuf.at[h, xs[d]], srow_a.at[h, d], ta_ssem.at[h], ta_rsem.at[h], x_line[d])
-            send(sbuf.at[h, :, ys[d]], srow_b.at[h, d], tb_ssem.at[h], tb_rsem.at[h], y_line[d])
-        for d in range(NX - 1):
-            send(obuf.at[h, 0, xs[d]], part_a.at[h, d], a_ssem.at[h], a_rsem.at[h], x_line[d])
-            send(obuf.at[h, 1, :, ys[d]], part_b.at[h, d], b_ssem.at[h], b_rsem.at[h], y_line[d])
-
-    def first_step(h):
-        wait_bytes(srow_a.at[h], ta_rsem.at[h])
-        weights_a, whole_a = merge_rows([sbuf[h, x]] + [srow_a[h, d] for d in range(NX - 1)])
-        srow2_a[h] = whole_a
-        wait_bytes(srow_b.at[h], tb_rsem.at[h])
-        weights_b, whole_b = merge_rows([sbuf[h, :, y]] + [srow_b[h, d] for d in range(NY - 1)])
-        srow2_b[h] = whole_b
-        for d in range(NX - 1):
-            send(srow2_a.at[h, ys[d]], sgot_a.at[h, d], ta2_ssem.at[h], ta2_rsem.at[h], y_line[d])
-            send(srow2_b.at[h, xs[d]], sgot_b.at[h, d], tb2_ssem.at[h], tb2_rsem.at[h], x_line[d])
-        wait_bytes(part_a.at[h], a_rsem.at[h])
-        parts = [obuf[h, 0, x]] + [part_a[h, d] for d in range(NX - 1)]
-        send_a[h] = weighted(weights_a, parts).astype(jnp.bfloat16)
-        wait_bytes(part_b.at[h], b_rsem.at[h])
-        parts = [obuf[h, 1, :, y]] + [part_b[h, d] for d in range(NY - 1)]
-        send_b[h] = weighted(weights_b, parts).astype(jnp.bfloat16)
-        for d in range(NX - 1):
-            send(send_a.at[h, ys[d]], got_a.at[h, d], a2_ssem.at[h], a2_rsem.at[h], y_line[d])
-            send(send_b.at[h, xs[d]], got_b.at[h, d], b2_ssem.at[h], b2_rsem.at[h], x_line[d])
+                lanes = slice(half * DH, half * DH + DH)
+                out = (maps[rows, lanes] * inverse[rows]).reshape(2, 16, DH).astype(jnp.bfloat16)
+                obuf[h, b // 2, (b % 2) * 2 : (b % 2) * 2 + 2, :, lanes] = out
+        for d, (xx, yy, to) in enumerate(plane):
+            send(sbuf.at[h, xx, yy], part_row.at[h, d], pr_ssem.at[h], pr_rsem.at[h], to)
+            send(obuf.at[h, xx, yy], part.at[h, d], p_ssem.at[h], p_rsem.at[h], to)
 
     def owner_of(h):
         return lax.rem(3 * h + HALF_Z - core, HALF_Z)
 
-    def second_step(h):
-        wait_bytes(sgot_a.at[h], ta2_rsem.at[h])
-        wait_bytes(sgot_b.at[h], tb2_rsem.at[h])
-        weights_a, whole_a = merge_rows([srow2_a[h, y]] + [sgot_a[h, d] for d in range(NY - 1)])
-        weights_b, _ = merge_rows([srow2_b[h, x]] + [sgot_b[h, d] for d in range(NX - 1)])
-        zsrow[h] = whole_a
-        wait_bytes(got_a.at[h], a2_rsem.at[h])
-        parts = [send_a[h, y]] + [got_a[h, d] for d in range(NY - 1)]
-        zsend[h, :, :DH] = weighted(weights_a, parts).astype(jnp.bfloat16)
-        wait_bytes(got_b.at[h], b2_rsem.at[h])
-        parts = [send_b[h, x]] + [got_b[h, d] for d in range(NX - 1)]
-        zsend[h, :, DH:] = weighted(weights_b, parts).astype(jnp.bfloat16)
+    def reduce(h):
+        count = NX * NY - 1
+        wait_bytes(part_row.at[h], pr_rsem.at[h])
+        weights, whole = merge_rows([sbuf[h, x, y]] + [part_row[h, d] for d in range(count)])
+        zsrow[h] = whole
+        wait_bytes(part.at[h], p_rsem.at[h])
+        merged = weighted(weights, [obuf[h, x, y]] + [part[h, d] for d in range(count)])
+        zsend[h] = merged.astype(jnp.bfloat16)
         for i in range(2):
             owner = owner_of(h) + i * HALF_Z
             gap = wrap(owner - z + NZ, NZ)
@@ -277,27 +254,23 @@
         def _():
             attend(i)
 
-        for step in range(2):
-
-            @pl.when(i == LAG + step)
-            def _():
-                pl.semaphore_wait(token_sem.at[step], 2)
-                token(step + 1)
-
-        @pl.when(i == 2 * LAG)
+        @pl.when(i == 0)
+        def _():
+            pl.semaphore_wait(token_sem.at[1], 2)
+            token(2)
+
+        @pl.when(i == LAG)
         def _():
             pl.semaphore_wait(token_sem.at[2], 2)
 
-        @pl.when(jnp.logical_and(i >= LAG, i < HEADS + LAG))
+        @pl.when(i >= LAG)
         def _():
-            first_step(i - LAG)
-
-        @pl.when(i >= 2 * LAG)
-        def _():
-            second_step(i - 2 * LAG)
+            reduce(i - LAG)
 
     own_q.wait()
-    loop(HEADS + 2 * LAG, turn_of)
+    pl.semaphore_wait(token_sem.at[0], 2)
+    token(1)
+    loop(HEADS + LAG, turn_of)
 
     mine = lax.rem(3 * (z + core), HALF_Z)
     is_owner = mine < HEADS
@@ -350,11 +323,8 @@
         for copy in pushes(h):
             copy.wait_send()
         wait_bytes(queries_of(h), q_ssem.at[h])
-        for part, sem in (
-            (part_a, a_ssem), (part_b, b_ssem), (srow_a, ta_ssem), (srow_b, tb_ssem),
-            (got_a, a2_ssem), (got_b, b2_ssem), (sgot_a, ta2_ssem), (sgot_b, tb2_ssem),
-        ):
-            wait_bytes(part.at[h], sem.at[h])
+        wait_bytes(part.at[h], p_ssem.at[h])
+        wait_bytes(part_row.at[h], pr_ssem.at[h])
 
         for i in range(2):
 
@@ -396,20 +366,10 @@
             pltpu.VMEM((256, 2 * KEYS), bf16),
             pltpu.VMEM((256, 128), f32),
             pltpu.VMEM((256, WIDE), f32),
-            pltpu.VMEM((HEADS, 2, NX, NY, 16, DH), bf16),
+            pltpu.VMEM((HEADS, NX, NY, 16, WIDE), bf16),
             pltpu.VMEM((HEADS, NX, NY, 1, 128), f32),
-            pltpu.VMEM((HEADS, NX - 1, NY, 16, DH), bf16),
-            pltpu.VMEM((HEADS, NY - 1, NX, 16, DH), bf16),
-            pltpu.VMEM((HEADS, NX - 1, NY, 1, 128), f32),
-            pltpu.VMEM((HEADS, NY - 1, NX, 1, 128), f32),
-            pltpu.VMEM((HEADS, NY, 16, DH), bf16),
-            pltpu.VMEM((HEADS, NX, 16, DH), bf16),
-            pltpu.VMEM((HEADS, NY, 1, 128), f32),
-            pltpu.VMEM((HEADS, NX, 1, 128), f32),
-            pltpu.VMEM((HEADS, NY - 1, 16, DH), bf16),
-            pltpu.VMEM((HEADS, NX - 1, 16, DH), bf16),
-            pltpu.VMEM((HEADS, NY - 1, 1, 128), f32),
-            pltpu.VMEM((HEADS, NX - 1, 1, 128), f32),
+            pltpu.VMEM((HEADS, NX * NY - 1, 16, WIDE), bf16),
+            pltpu.VMEM((HEADS, NX * NY - 1, 1, 128), f32),
             pltpu.VMEM((HEADS, 16, WIDE), bf16),
             pltpu.VMEM((HEADS, 1, 128), f32),
             pltpu.VMEM((NZ - 1, 16, WIDE), bf16),
@@ -417,8 +377,7 @@
             pltpu.VMEM((4 * HEADS, 16, DH), bf16),
             dma((3,)), heads, heads, dma,
             heads, heads, heads, heads, heads, heads,
-            heads, heads, heads, heads, heads, heads, heads, heads,
-            heads, heads, heads, heads, heads, heads, heads, heads,
+            heads, heads, heads, heads,
             dma((HEADS, 2)), dma, dma((HEADS, 2)), dma, dma((4,)), dma,
             pltpu.SemaphoreType.REGULAR((3,)),
         ],

time: 52.3 us -> 49.6 us (0.948)
  Pallas kernels: 50 us -> 47.2 us
    pallas_call x1, Pallas kernels: 50 us -> 47.2 us  [per_device(): pl.pallas_call(kernel, out_shape=jax.ShapeDtypeStruct((row_count, width),...]
where the time goes in v3:
time: 49.6 us; the launch traced here: 49.4 us
  Pallas kernels  47.2 us (95%)
  local copies, waits for them, and re-layouts  1.53 us (3%)
  between operations  0.66 us (1%)
    pallas_call x1, Pallas kernels, per_device(): pl.pallas_call(kernel, out_shape=jax.ShapeDtypeStruct((row_count, width),...  47.2 us
    unnamed x1, local copies, waits for them, and re-layouts  1.53 us

profile of v3, /device:TPU:1, one launch (start us, length us, event | category | flops | bytes accessed | tf_op | source)
XLA Modules:
  0.0 49.4 jit_solution(3500319642929188717)
XLA Ops:
  0.7 47.2 %shard_map.64 = bf16[16,2560]{1,0:T(8,128)(2,1)} custom-call(s32[1]{0:T(128)S(6)} %copy.8.offset_hbm, f32[10]{0:T(128)} %lam_hbm.1, f32[2560]{0:T(1024)} %gain_hbm.1, bf16[16,2560]{1,0:T(8,128)(2,1)} %q_ref.1, bf16[384,2560]{1,0:T(8,128)(2,1)} %k_ref.1, bf16[384,2560]{1,0:T(8,128)(2,1)} %v_ref.1), custom_call_target="tpu_custom_call" | custom-call | flops 800000000 | bytes 8000000 | tf_op jit(solution)/shard_map/pallas_call | solution.py:351
  47.9 1.5 %copy.9 = bf16[16,2560]{1,0:T(8,128)(2,1)} copy(bf16[16,2560]{1,0:T(8,128)(2,1)} %shard_map.64) | data formatting | bytes 163840

commit v4 on v3

--- a/solution.py
+++ b/solution.py
@@ -190,32 +190,48 @@
 
     scale = DH ** (-0.5) * math.log2(math.e)
 
-    def attend(h):
-        own_k, own_v = own_copies(h)
+    blocks = [slice(32 * b, 32 * b + 32) for b in range(8)]
+
+    def prepare(h):
         wait_bytes(queries_of(h), q_rsem.at[h])
-        blocks = [slice(32 * b, 32 * b + 32) for b in range(8)]
         lane = lax.broadcasted_iota(jnp.int32, (2, CHUNK, WIDE), 2)
         for b, rows in enumerate(blocks):
             q = qbuf[b, :, cols(0, h)].astype(jnp.float32).reshape(2, CHUNK, WIDE)
             both = jnp.concatenate([jnp.where(lane < DH, q, 0.0), jnp.where(lane >= DH, q, 0.0)], axis=1)
-            tall[rows] = both.reshape(32, WIDE).astype(jnp.bfloat16)
-        own_k.wait()
+            tall[h % 2, rows] = both.reshape(32, WIDE).astype(jnp.bfloat16)
+        own_copies(h)[0].wait()
         wait_bytes(kbuf.at[h, pl.ds(KEYS, KEYS)], k_rsem.at[h])
-        scores[...] = lax.dot_general(
-            tall[...], kbuf[h], (((1,), (1,)), ((), ())), preferred_element_type=jnp.float32
+
+    def score(h, tile):
+        keys = slice(256 * tile, 256 * tile + 256)
+        scores[h % 2, :, keys] = lax.dot_general(
+            tall[h % 2], kbuf[h, keys], (((1,), (1,)), ((), ())), preferred_element_type=jnp.float32
         )
-        stat_lane = lax.broadcasted_iota(jnp.int32, (2, 16, 128), 2)
-        stat_sub = lax.broadcasted_iota(jnp.int32, (2, 16, 128), 1)
-        for b, rows in enumerate(blocks):
-            score = scores[rows] * scale + bias[rows]
-            top = jnp.max(score, axis=1, keepdims=True)
-            e = jnp.exp2(score - top)
-            total = jnp.sum(e, axis=1, keepdims=True)
-            expo[rows] = e.astype(jnp.bfloat16)
-            inverse[rows] = jnp.broadcast_to(1.0 / total, (32, 128))
-            stat = jnp.broadcast_to((top + jnp.log2(total)).reshape(2, 16, 1), (2, 16, 128))
-            stat = jnp.where(stat_lane == stat_sub, stat, 0.0)
-            sbuf[h, b // 2, (b % 2) * 2 : (b % 2) * 2 + 2] = jnp.sum(stat, axis=1, keepdims=True)
+
+    stat_lane = lax.broadcasted_iota(jnp.int32, (2, 16, 128), 2)
+    stat_sub = lax.broadcasted_iota(jnp.int32, (2, 16, 128), 1)
+
+    def soften(h, b):
+        rows = blocks[b]
+        values = scores[h % 2, rows] * scale + bias[rows]
+        top = jnp.max(values, axis=1, keepdims=True)
+        e = jnp.exp2(values - top)
+        total = jnp.sum(e, axis=1, keepdims=True)
+        expo[rows] = e.astype(jnp.bfloat16)
+        inverse[rows] = jnp.broadcast_to(1.0 / total, (32, 128))
+        stat = jnp.broadcast_to((top + jnp.log2(total)).reshape(2, 16, 1), (2, 16, 128))
+        stat = jnp.where(stat_lane == stat_sub, stat, 0.0)
+        sbuf[h, b // 2, (b % 2) * 2 : (b % 2) * 2 + 2] = jnp.sum(stat, axis=1, keepdims=True)
+
+    def attend(h):
+        own_v = own_copies(h)[1]
+        if h + 1 < HEADS:
+            prepare(h + 1)
+        for tile, some in enumerate(((0, 1, 2), (3, 4, 5), (6, 7))):
+            if h + 1 < HEADS:
+                score(h + 1, tile)
+            for b in some:
+                soften(h, b)
         own_v.wait()
         wait_bytes(vbuf.at[h, pl.ds(KEYS, KEYS)], v_rsem.at[h])
         maps[...] = jnp.dot(expo[...], vbuf[h], preferred_element_type=jnp.float32)
@@ -249,28 +265,22 @@
                 send(zsrow.at[h], zsbuf.at[gap - 1], zt_ssem.at[h, i], zt_rsem, to)
                 send(zsend.at[h], zbuf.at[gap - 1], z_ssem.at[h, i], z_rsem, to)
 
-    def turn_of(i):
-        @pl.when(i < HEADS)
-        def _():
-            attend(i)
-
-        @pl.when(i == 0)
-        def _():
-            pl.semaphore_wait(token_sem.at[1], 2)
-            token(2)
-
-        @pl.when(i == LAG)
-        def _():
-            pl.semaphore_wait(token_sem.at[2], 2)
-
-        @pl.when(i >= LAG)
-        def _():
-            reduce(i - LAG)
-
     own_q.wait()
     pl.semaphore_wait(token_sem.at[0], 2)
     token(1)
-    loop(HEADS + LAG, turn_of)
+    prepare(0)
+    for tile in range(3):
+        score(0, tile)
+    for i in range(HEADS + LAG):
+        if i < HEADS:
+            attend(i)
+        if i == 0:
+            pl.semaphore_wait(token_sem.at[1], 2)
+            token(2)
+        if i == LAG:
+            pl.semaphore_wait(token_sem.at[2], 2)
+        if i >= LAG:
+            reduce(i - LAG)
 
     mine = lax.rem(3 * (z + core), HALF_Z)
     is_owner = mine < HEADS
@@ -361,8 +371,8 @@
             pltpu.VMEM((HEADS, 2 * KEYS, WIDE), bf16),
             pltpu.VMEM((8, 16, HEADS * WIDE), bf16),
             pltpu.VMEM((256, 2 * KEYS), f32),
-            pltpu.VMEM((256, WIDE), bf16),
-            pltpu.VMEM((256, 2 * KEYS), f32),
+            pltpu.VMEM((2, 256, WIDE), bf16),
+            pltpu.VMEM((2, 256, 2 * KEYS), f32),
             pltpu.VMEM((256, 2 * KEYS), bf16),
             pltpu.VMEM((256, 128), f32),
             pltpu.VMEM((256, WIDE), f32),

time: 49.6 us -> 49.7 us (level)
  no operation moved by 1% of the time
where the time goes in v4:
time: 49.7 us; the launch traced here: 49.5 us
  Pallas kernels  47.3 us (95%)
  local copies, waits for them, and re-layouts  1.53 us (3%)
  between operations  0.66 us (1%)
    pallas_call x1, Pallas kernels, per_device(): pl.pallas_call(kernel, out_shape=jax.ShapeDtypeStruct((row_count, width),...  47.3 us
    unnamed x1, local copies, waits for them, and re-layouts  1.53 us

profile of v4, /device:TPU:1, one launch (start us, length us, event | category | flops | bytes accessed | tf_op | source)
XLA Modules:
  0.0 49.5 jit_solution(3160506424351013182)
XLA Ops:
  0.7 47.3 %shard_map.64 = bf16[16,2560]{1,0:T(8,128)(2,1)} custom-call(s32[1]{0:T(128)S(6)} %copy.8.offset_hbm, f32[10]{0:T(128)} %lam_hbm.1, f32[2560]{0:T(1024)} %gain_hbm.1, bf16[16,2560]{1,0:T(8,128)(2,1)} %q_ref.1, bf16[384,2560]{1,0:T(8,128)(2,1)} %k_ref.1, bf16[384,2560]{1,0:T(8,128)(2,1)} %v_ref.1), custom_call_target="tpu_custom_call" | custom-call | flops 800000000 | bytes 8000000 | tf_op jit(solution)/shard_map/pallas_call | solution.py:361
  48.0 1.5 %copy.9 = bf16[16,2560]{1,0:T(8,128)(2,1)} copy(bf16[16,2560]{1,0:T(8,128)(2,1)} %shard_map.64) | data formatting | bytes 163840

commit v5 on v4

--- a/solution.py
+++ b/solution.py
@@ -21,6 +21,7 @@
 
 
 LAG = 2
+TWO = 3
 
 
 def wrap(index, size):
@@ -75,9 +76,12 @@
     offset_hbm, lam_hbm, gain_hbm, q_ref, k_ref, v_ref, out_ref,
     offset_ref, lam_ref, gain_ref,
     kbuf, vbuf, qbuf, bias, tall, scores, expo, inverse, maps, obuf, sbuf, part, part_row,
+    part_a, part_b, srow_a, srow_b, send_a, send_b, srow2_a, srow2_b, got_a, got_b, sgot_a, sgot_b,
     zsend, zsrow, zbuf, zsbuf, fin,
     small_sem, kl_sem, vl_sem, ql_sem, k_ssem, k_rsem, v_ssem, v_rsem, q_ssem, q_rsem,
     p_ssem, p_rsem, pr_ssem, pr_rsem,
+    a_ssem, a_rsem, b_ssem, b_rsem, ta_ssem, ta_rsem, tb_ssem, tb_rsem,
+    a2_ssem, a2_rsem, b2_ssem, b2_rsem, ta2_ssem, ta2_rsem, tb2_ssem, tb2_rsem,
     z_ssem, z_rsem, zt_ssem, zt_rsem, g_ssem, g_rsem, token_sem,
 ):
     ctx = lax.axis_index("ctx")
@@ -101,6 +105,7 @@
         for j, yy in enumerate([y] + ys)
     ][1:]
     x_line = [(ctx, xx * 2 + y_hi) for xx in xs]
+    y_line = [(c, x * 2 + hi) for c, hi in zip(ctx_of, hi_of)][1:]
     mirror = [(pair[0], xx * 2 + 1 - y_hi) for xx in [x] + xs]
     z_base = y_lo * 2 * NZ + core
 
@@ -240,21 +245,72 @@
                 lanes = slice(half * DH, half * DH + DH)
                 out = (maps[rows, lanes] * inverse[rows]).reshape(2, 16, DH).astype(jnp.bfloat16)
                 obuf[h, b // 2, (b % 2) * 2 : (b % 2) * 2 + 2, :, lanes] = out
+        if h < TWO:
+            for d in range(NX - 1):
+                send(sbuf.at[h, xs[d]], srow_a.at[h, d], ta_ssem.at[h], ta_rsem.at[h], x_line[d])
+                send(sbuf.at[h, :, ys[d]], srow_b.at[h, d], tb_ssem.at[h], tb_rsem.at[h], y_line[d])
+            for d in range(NX - 1):
+                send(
+                    obuf.at[h, xs[d], :, :, pl.ds(0, DH)], part_a.at[h, d],
+                    a_ssem.at[h], a_rsem.at[h], x_line[d],
+                )
+                send(
+                    obuf.at[h, :, ys[d], :, pl.ds(DH, DH)], part_b.at[h, d],
+                    b_ssem.at[h], b_rsem.at[h], y_line[d],
+                )
+            return
         for d, (xx, yy, to) in enumerate(plane):
-            send(sbuf.at[h, xx, yy], part_row.at[h, d], pr_ssem.at[h], pr_rsem.at[h], to)
-            send(obuf.at[h, xx, yy], part.at[h, d], p_ssem.at[h], p_rsem.at[h], to)
+            send(sbuf.at[h, xx, yy], part_row.at[h - TWO, d], pr_ssem.at[h], pr_rsem.at[h], to)
+            send(obuf.at[h, xx, yy], part.at[h - TWO, d], p_ssem.at[h], p_rsem.at[h], to)
+
+    def first_step(h):
+        wait_bytes(srow_a.at[h], ta_rsem.at[h])
+        weights_a, whole_a = merge_rows([sbuf[h, x]] + [srow_a[h, d] for d in range(NX - 1)])
+        srow2_a[h] = whole_a
+        wait_bytes(srow_b.at[h], tb_rsem.at[h])
+        weights_b, whole_b = merge_rows([sbuf[h, :, y]] + [srow_b[h, d] for d in range(NY - 1)])
+        srow2_b[h] = whole_b
+        for d in range(NX - 1):
+            send(srow2_a.at[h, ys[d]], sgot_a.at[h, d], ta2_ssem.at[h], ta2_rsem.at[h], y_line[d])
+            send(srow2_b.at[h, xs[d]], sgot_b.at[h, d], tb2_ssem.at[h], tb2_rsem.at[h], x_line[d])
+        wait_bytes(part_a.at[h], a_rsem.at[h])
+        parts = [obuf[h, x, :, :, :DH]] + [part_a[h, d] for d in range(NX - 1)]
+        send_a[h] = weighted(weights_a, parts).astype(jnp.bfloat16)
+        wait_bytes(part_b.at[h], b_rsem.at[h])
+        parts = [obuf[h, :, y, :, DH:]] + [part_b[h, d] for d in range(NY - 1)]
+        send_b[h] = weighted(weights_b, parts).astype(jnp.bfloat16)
+        for d in range(NX - 1):
+            send(send_a.at[h, ys[d]], got_a.at[h, d], a2_ssem.at[h], a2_rsem.at[h], y_line[d])
+            send(send_b.at[h, xs[d]], got_b.at[h, d], b2_ssem.at[h], b2_rsem.at[h], x_line[d])
+
+    def second_step(h):
+        wait_bytes(sgot_a.at[h], ta2_rsem.at[h])
+        wait_bytes(sgot_b.at[h], tb2_rsem.at[h])
+        weights_a, whole_a = merge_rows([srow2_a[h, y]] + [sgot_a[h, d] for d in range(NY - 1)])
+        weights_b, _ = merge_rows([srow2_b[h, x]] + [sgot_b[h, d] for d in range(NX - 1)])
+        zsrow[h] = whole_a
+        wait_bytes(got_a.at[h], a2_rsem.at[h])
+        parts = [send_a[h, y]] + [got_a[h, d] for d in range(NY - 1)]
+        zsend[h, :, :DH] = weighted(weights_a, parts).astype(jnp.bfloat16)
+        wait_bytes(got_b.at[h], b2_rsem.at[h])
+        parts = [send_b[h, x]] + [got_b[h, d] for d in range(NX - 1)]
+        zsend[h, :, DH:] = weighted(weights_b, parts).astype(jnp.bfloat16)
+        hand_over(h)
 
     def owner_of(h):
         return lax.rem(3 * h + HALF_Z - core, HALF_Z)
 
     def reduce(h):
         count = NX * NY - 1
-        wait_bytes(part_row.at[h], pr_rsem.at[h])
-        weights, whole = merge_rows([sbuf[h, x, y]] + [part_row[h, d] for d in range(count)])
+        wait_bytes(part_row.at[h - TWO], pr_rsem.at[h])
+        weights, whole = merge_rows([sbuf[h, x, y]] + [part_row[h - TWO, d] for d in range(count)])
         zsrow[h] = whole
-        wait_bytes(part.at[h], p_rsem.at[h])
-        merged = weighted(weights, [obuf[h, x, y]] + [part[h, d] for d in range(count)])
+        wait_bytes(part.at[h - TWO], p_rsem.at[h])
+        merged = weighted(weights, [obuf[h, x, y]] + [part[h - TWO, d] for d in range(count)])
         zsend[h] = merged.astype(jnp.bfloat16)
+        hand_over(h)
+
+    def hand_over(h):
         for i in range(2):
             owner = owner_of(h) + i * HALF_Z
             gap = wrap(owner - z + NZ, NZ)
@@ -279,7 +335,11 @@
             token(2)
         if i == LAG:
             pl.semaphore_wait(token_sem.at[2], 2)
-        if i >= LAG:
+        if LAG <= i < TWO + LAG:
+            first_step(i - LAG)
+        if 2 * LAG <= i < TWO + 2 * LAG:
+            second_step(i - 2 * LAG)
+        if TWO + LAG <= i:
             reduce(i - LAG)
 
     mine = lax.rem(3 * (z + core), HALF_Z)
@@ -333,8 +393,6 @@
         for copy in pushes(h):
             copy.wait_send()
         wait_bytes(queries_of(h), q_ssem.at[h])
-        wait_bytes(part.at[h], p_ssem.at[h])
-        wait_bytes(part_row.at[h], pr_ssem.at[h])
 
         for i in range(2):
 
@@ -344,6 +402,15 @@
                 wait_bytes(zsrow.at[h], zt_ssem.at[h, i])
 
     loop(HEADS, left)
+    for h in range(TWO, HEADS):
+        wait_bytes(part.at[h - TWO], p_ssem.at[h])
+        wait_bytes(part_row.at[h - TWO], pr_ssem.at[h])
+    for h in range(TWO):
+        for landed, sem in (
+            (part_a, a_ssem), (part_b, b_ssem), (srow_a, ta_ssem), (srow_b, tb_ssem),
+            (got_a, a2_ssem), (got_b, b2_ssem), (sgot_a, ta2_ssem), (sgot_b, tb2_ssem),
+        ):
+            wait_bytes(landed.at[h], sem.at[h])
     @pl.when(is_owner)
     def _():
         wait_bytes(fin.at[pl.ds(0, HALF_Z - 1)], g_ssem.at[0])
@@ -378,8 +445,20 @@
             pltpu.VMEM((256, WIDE), f32),
             pltpu.VMEM((HEADS, NX, NY, 16, WIDE), bf16),
             pltpu.VMEM((HEADS, NX, NY, 1, 128), f32),
-            pltpu.VMEM((HEADS, NX * NY - 1, 16, WIDE), bf16),
-            pltpu.VMEM((HEADS, NX * NY - 1, 1, 128), f32),
+            pltpu.VMEM((HEADS - TWO, NX * NY - 1, 16, WIDE), bf16),
+            pltpu.VMEM((HEADS - TWO, NX * NY - 1, 1, 128), f32),
+            pltpu.VMEM((TWO, NX - 1, NY, 16, DH), bf16),
+            pltpu.VMEM((TWO, NY - 1, NX, 16, DH), bf16),
+            pltpu.VMEM((TWO, NX - 1, NY, 1, 128), f32),
+            pltpu.VMEM((TWO, NY - 1, NX, 1, 128), f32),
+            pltpu.VMEM((TWO, NY, 16, DH), bf16),
+            pltpu.VMEM((TWO, NX, 16, DH), bf16),
+            pltpu.VMEM((TWO, NY, 1, 128), f32),
+            pltpu.VMEM((TWO, NX, 1, 128), f32),
+            pltpu.VMEM((TWO, NY - 1, 16, DH), bf16),
+            pltpu.VMEM((TWO, NX - 1, 16, DH), bf16),
+            pltpu.VMEM((TWO, NY - 1, 1, 128), f32),
+            pltpu.VMEM((TWO, NX - 1, 1, 128), f32),
             pltpu.VMEM((HEADS, 16, WIDE), bf16),
             pltpu.VMEM((HEADS, 1, 128), f32),
             pltpu.VMEM((NZ - 1, 16, WIDE), bf16),
@@ -388,6 +467,8 @@
             dma((3,)), heads, heads, dma,
             heads, heads, heads, heads, heads, heads,
             heads, heads, heads, heads,
+            heads, heads, heads, heads, heads, heads, heads, heads,
+            heads, heads, heads, heads, heads, heads, heads, heads,
             dma((HEADS, 2)), dma, dma((HEADS, 2)), dma, dma((4,)), dma,
             pltpu.SemaphoreType.REGULAR((3,)),
         ],

time: 49.7 us -> 50.3 us (1.012)
  Pallas kernels: 47.3 us -> 47.9 us
    pallas_call x1, Pallas kernels: 47.3 us -> 47.9 us  [per_device(): pl.pallas_call(kernel, out_shape=jax.ShapeDtypeStruct((row_count, width),...]
where the time goes in v5:
time: 50.3 us; the launch traced here: 50.1 us
  Pallas kernels  47.9 us (95%)
  local copies, waits for them, and re-layouts  1.53 us (3%)
  between operations  0.66 us (1%)
    pallas_call x1, Pallas kernels, per_device(): pl.pallas_call(kernel, out_shape=jax.ShapeDtypeStruct((row_count, width),...  47.9 us
    unnamed x1, local copies, waits for them, and re-layouts  1.53 us

profile of v5, /device:TPU:1, one launch (start us, length us, event | category | flops | bytes accessed | tf_op | source)
XLA Modules:
  0.0 50.1 jit_solution(707690066153178515)
XLA Ops:
  0.7 47.9 %shard_map.64 = bf16[16,2560]{1,0:T(8,128)(2,1)} custom-call(s32[1]{0:T(128)S(6)} %copy.8.offset_hbm, f32[10]{0:T(128)} %lam_hbm.1, f32[2560]{0:T(1024)} %gain_hbm.1, bf16[16,2560]{1,0:T(8,128)(2,1)} %q_ref.1, bf16[384,2560]{1,0:T(8,128)(2,1)} %k_ref.1, bf16[384,2560]{1,0:T(8,128)(2,1)} %v_ref.1), custom_call_target="tpu_custom_call" | custom-call | flops 800000000 | bytes 8000000 | tf_op jit(solution)/shard_map/pallas_call | solution.py:428
  48.6 1.5 %copy.9 = bf16[16,2560]{1,0:T(8,128)(2,1)} copy(bf16[16,2560]{1,0:T(8,128)(2,1)} %shard_map.64) | data formatting | bytes 163840

commit v6 on v3

--- a/solution.py
+++ b/solution.py
@@ -100,6 +100,8 @@
         for xx in [x] + xs
         for j, yy in enumerate([y] + ys)
     ][1:]
+    hops = (0, 1, 2, 1)
+    far_first = sorted(range(NX * NY - 1), key=lambda d: -hops[(d + 1) // NY] - hops[(d + 1) % NY])
     x_line = [(ctx, xx * 2 + y_hi) for xx in xs]
     mirror = [(pair[0], xx * 2 + 1 - y_hi) for xx in [x] + xs]
     z_base = y_lo * 2 * NZ + core
@@ -167,7 +169,7 @@
 
     def push_head(h):
         mine = q_ref.at[:, cols(core, h)]
-        for to in mirror + x_line:
+        for to in (mirror[2], x_line[1], mirror[1], mirror[3], x_line[0], x_line[2], mirror[0]):
             send(mine, qbuf.at[blk, :, cols(0, h)], q_ssem.at[h], q_rsem.at[h], to)
         push(h)
 
@@ -224,7 +226,8 @@
                 lanes = slice(half * DH, half * DH + DH)
                 out = (maps[rows, lanes] * inverse[rows]).reshape(2, 16, DH).astype(jnp.bfloat16)
                 obuf[h, b // 2, (b % 2) * 2 : (b % 2) * 2 + 2, :, lanes] = out
-        for d, (xx, yy, to) in enumerate(plane):
+        for d in far_first:
+            xx, yy, to = plane[d]
             send(sbuf.at[h, xx, yy], part_row.at[h, d], pr_ssem.at[h], pr_rsem.at[h], to)
             send(obuf.at[h, xx, yy], part.at[h, d], p_ssem.at[h], p_rsem.at[h], to)
 
@@ -272,6 +275,21 @@
     token(1)
     loop(HEADS + LAG, turn_of)
 
+    def left(h):
+        for copy in pushes(h):
+            copy.wait_send()
+        wait_bytes(queries_of(h), q_ssem.at[h])
+        wait_bytes(part.at[h], p_ssem.at[h])
+        wait_bytes(part_row.at[h], pr_ssem.at[h])
+
+        for i in range(2):
+
+            @pl.when(owner_of(h) + i * HALF_Z != z)
+            def _():
+                wait_bytes(zsend.at[h], z_ssem.at[h, i])
+                wait_bytes(zsrow.at[h], zt_ssem.at[h, i])
+
+    loop(HEADS, left)
     mine = lax.rem(3 * (z + core), HALF_Z)
     is_owner = mine < HEADS
     all_tiles = 4 * HEADS
@@ -319,21 +337,6 @@
 
     loop(HEADS, assemble)
 
-    def left(h):
-        for copy in pushes(h):
-            copy.wait_send()
-        wait_bytes(queries_of(h), q_ssem.at[h])
-        wait_bytes(part.at[h], p_ssem.at[h])
-        wait_bytes(part_row.at[h], pr_ssem.at[h])
-
-        for i in range(2):
-
-            @pl.when(owner_of(h) + i * HALF_Z != z)
-            def _():
-                wait_bytes(zsend.at[h], z_ssem.at[h, i])
-                wait_bytes(zsrow.at[h], zt_ssem.at[h, i])
-
-    loop(HEADS, left)
     @pl.when(is_owner)
     def _():
         wait_bytes(fin.at[pl.ds(0, HALF_Z - 1)], g_ssem.at[0])

time: 49.6 us -> 48.7 us (0.982)
  Pallas kernels: 47.2 us -> 46.4 us
    pallas_call x1, Pallas kernels: 47.2 us -> 46.4 us  [per_device(): pl.pallas_call(kernel, out_shape=jax.ShapeDtypeStruct((row_count, width),...]
where the time goes in v6:
time: 48.7 us; the launch traced here: 48.6 us
  Pallas kernels  46.4 us (95%)
  local copies, waits for them, and re-layouts  1.53 us (3%)
  between operations  0.66 us (1%)
    pallas_call x1, Pallas kernels, per_device(): pl.pallas_call(kernel, out_shape=jax.ShapeDtypeStruct((row_count, width),...  46.4 us
    unnamed x1, local copies, waits for them, and re-layouts  1.53 us

profile of v6, /device:TPU:1, one launch (start us, length us, event | category | flops | bytes accessed | tf_op | source)
XLA Modules:
  0.0 48.6 jit_solution(18440246082289010019)
XLA Ops:
  0.7 46.4 %shard_map.64 = bf16[16,2560]{1,0:T(8,128)(2,1)} custom-call(s32[1]{0:T(128)S(6)} %copy.8.offset_hbm, f32[10]{0:T(128)} %lam_hbm.1, f32[2560]{0:T(1024)} %gain_hbm.1, bf16[16,2560]{1,0:T(8,128)(2,1)} %q_ref.1, bf16[384,2560]{1,0:T(8,128)(2,1)} %k_ref.1, bf16[384,2560]{1,0:T(8,128)(2,1)} %v_ref.1), custom_call_target="tpu_custom_call" | custom-call | flops 800000000 | bytes 8000000 | tf_op jit(solution)/shard_map/pallas_call | solution.py:354
  47.1 1.5 %copy.9 = bf16[16,2560]{1,0:T(8,128)(2,1)} copy(bf16[16,2560]{1,0:T(8,128)(2,1)} %shard_map.64) | data formatting | bytes 163840
